TPU v7x, 32 devices: a whole 2x2x4 slice. The times are simulated.
32 devices in a mesh: gx: 8 (over z, y), gy: 4 (over x, core).
Axes of the slice: x: 2, y: 2, z: 4, core: 2. Of those that a mesh axis runs over, the one named last changes fastest.
Arguments:
- cell_means: float32 [30, 32, 16, 128], P(None, 'gx', 'gy'), may hold values from 0 to 1
- diffusion: float32 [32, 16, 128], P('gx', 'gy'), may hold values from 0.02 to 0.15
- mix_rate: float32 [32, 16, 128], P('gx', 'gy'), may hold values from 0.05 to 3
- send_lists: int32 [32, 32, 128], P(('gx', 'gy')), may hold values from 0 to 2047
- compositions: float32 [30, 131072], P(None, ('gx', 'gy')), may hold values from 0 to 1
- weights: float32 [131072], P(('gx', 'gy')), may hold values from 0.5 to 2
- particle_slots: int32 [131072], P(('gx', 'gy')), may hold values from 0 to 4095
- partners: int32 [131072], P(('gx', 'gy')), may hold values from 0 to 4095
Outputs:
- new_means: float32 [30, 32, 16, 128], P(None, 'gx', 'gy')
- new_compositions: float32 [30, 131072], P(None, ('gx', 'gy'))
Inputs may be any that keep to these rules, and one draw needn't show every extreme that they name: particle_slots = s * 128 + r names slot r of the list that tile s sends to the particle's device.
All inputs are finite; a program needn't handle non-finite values.
Results may differ from a plain program's by a relative error of at most 0.00002.
Values sent between devices are 32-bit elements; how exact they have to be, the bound alone decides.
A program may use at most 64 MiB of HBM per device.

v0:
```python
import jax
import jax.numpy as jnp
from jax import lax
from jax.sharding import PartitionSpec as P

PAIR_RATE = 0.3


def with_halo(shard, sides, width):
    for axis, dim in sides:
        devices, length = (lax.axis_size(axis), shard.shape[dim])
        up = [(i, (i + 1) % devices) for i in range(devices - 1)]
        down = [(j, i) for i, j in up]
        last = lax.slice_in_dim(shard, length - width, length, axis=dim)
        initial = lax.slice_in_dim(shard, 0, width, axis=dim)
        before = lax.ppermute(last, axis, up)
        after = lax.ppermute(initial, axis, down)
        shard = jnp.concatenate([before, shard, after], axis=dim)
    return shard


def on_device(
    cell_means, diffusion, mix_rate, send_lists, compositions, weights, particle_slots, partners
):
    species, rows_x, rows_y, depth = cell_means.shape
    cell_count = rows_x * rows_y * depth
    groups_x = lax.axis_size("gx")
    groups_y = lax.axis_size("gy")
    padded = with_halo(cell_means, (("gx", 1), ("gy", 2)), 1)
    deepened = jnp.pad(cell_means, ((0, 0), (0, 0), (0, 0), (1, 1)))
    neighbours = (
        padded[:, 2:, 1:-1] + padded[:, :-2, 1:-1] + padded[:, 1:-1, 2:] + padded[:, 1:-1, :-2]
    )
    neighbours = neighbours + deepened[:, :, :, 2:] + deepened[:, :, :, :-2]
    filtered = cell_means + diffusion[None] * (neighbours - 6.0 * cell_means)
    fields = jnp.concatenate(
        [filtered.reshape(species, cell_count), mix_rate.reshape(1, cell_count)], 0
    )
    slots_peer = send_lists.shape[2]
    slot_count = groups_x * groups_y * slots_peer
    flat_list = send_lists[0].reshape(-1)
    outgoing = jnp.take(fields, flat_list, axis=1)
    received = lax.all_to_all(outgoing, ("gx", "gy"), split_axis=1, concat_axis=1, tiled=True)
    local_means = jnp.take(received, particle_slots, axis=1)
    mates = jnp.take(compositions, partners, axis=1)
    blend_rate = 1.0 - jnp.exp(-local_means[species])
    new_compositions = (
        compositions
        - blend_rate[None] * (compositions - local_means[:species])
        - PAIR_RATE * (compositions - mates)
    )
    weighted = jnp.concatenate([weights[None] * new_compositions, weights[None]], 0)
    moments = jnp.zeros((species + 1, slot_count), jnp.float32).at[:, particle_slots].add(weighted)
    returned = lax.all_to_all(moments, ("gx", "gy"), split_axis=1, concat_axis=1, tiled=True)
    totals = jnp.zeros((species + 1, cell_count), jnp.float32).at[:, flat_list].add(returned)
    updated = (totals[:species] + fields[:species]) / (totals[species][None] + 1.0)
    return (updated.reshape(species, rows_x, rows_y, depth), new_compositions)


def solution(mesh):
    in_specs = (
        P(None, "gx", "gy", None),
        P("gx", "gy", None),
        P("gx", "gy", None),
        P(("gx", "gy"), None, None),
        P(None, ("gx", "gy")),
        P(("gx", "gy")),
        P(("gx", "gy")),
        P(("gx", "gy")),
    )
    out_specs = (P(None, "gx", "gy", None), P(None, ("gx", "gy")))
    return jax.shard_map(
        on_device, mesh=mesh, in_specs=in_specs, out_specs=out_specs, check_vma=False
    )
```

profile of v0, /device:TPU:0, one launch (start us, length us, event | category | flops | bytes accessed | tf_op | source)
XLA Modules:
  0.0 158.9 jit_solution(12772471050581777557)
XLA Ops:
  0.6 0.0 copy-start.2
  0.6 0.0 copy-start.6
  0.7 0.9 fusion.23
  1.6 4.9 %collective-permute-start.1 = (f32[30,1,4,128]{3,2,1,0:T(4,128)S(1)}, f32[30,1,4,128]{3,2,1,0:T(4,128)S(1)}, u32[]{:S(2)}, u32[]{:S(2)}) collective-permute-start(f32[30,1,4,128]{3,2,1,0:T(4,128)S(1)} %get-tuple-element.19), channel_id=1, source_target_pairs={{0,4},{4,8},{8,12},{12,16},{16,20},{20,24},{24,28},{1,5},{5,9},{9,... | collective-permute-start | bytes 184328 | tf_op jit(solution)/shard_map/ppermute | solution.py:16
  6.4 1.3 collective-permute-start
  7.7 0.7 compare_select_fusion
  8.5 0.0 collective-permute-done.1
  8.5 1.0 constant_dynamic-update-slice_fusion.1
  9.5 3.0 %collective-permute-done = f32[30,1,4,128]{3,2,1,0:T(4,128)S(1)} collective-permute-done((f32[30,1,4,128]{3,2,1,0:T(4,128)S(1)}, f32[30,1,4,128]{3,2,1,0:T(4,128)S(1)}, u32[]{:S(2)}, u32[]{:S(2)}) %collective-permute-start) | collective-permute-done | bytes 61472 | tf_op jit(solution)/shard_map/ppermute | solution.py:17
  12.6 0.1 fusion.22
  12.7 1.3 collective-permute-start.3
  14.0 1.3 collective-permute-start.2
  15.3 0.7 compare_and_fusion.1
  16.1 1.1 copy.72
  17.1 0.0 collective-permute-done.3
  17.1 1.8 %collective-permute-done.2 = f32[30,6,1,128]{3,2,1,0:T(1,128)S(1)} collective-permute-done((f32[30,6,1,128]{3,2,1,0:T(1,128)S(1)}, f32[30,6,1,128]{3,2,1,0:T(1,128)S(1)}, u32[]{:S(2)}, u32[]{:S(2)}) %collective-permute-start.2) | collective-permute-done | bytes 92192 | tf_op jit(solution)/shard_map/ppermute | solution.py:17
  18.9 0.0 copy-done.2
  19.0 0.0 copy-done.6
  19.0 0.4 fusion.14
  19.4 0.4 copy.71
  19.8 0.3 pad_maximum_fusion
  20.1 14.2 %gather_fusion = f32[4096,31]{1,0:T(8,128)} fusion(f32[31,2048]{0,1:T(8,128)S(1)} %pad_maximum_fusion, s32[4096]{0:T(1024)S(1)} %broadcast_clamp_fusion.1), kind=kCustom, calls=%fused_computation | custom fusion | bytes 1032192 | tf_op jit(solution)/shard_map/jit(_take)/gather | solution.py:42
  34.3 2.2 %copy.73 = f32[31,32,128]{2,0,1:T(8,128)S(1)} copy(f32[31,32,128]{0,2,1:T(8,128)} %bitcast.37) | data formatting | bytes 1015808 | tf_op jit(solution)/shard_map/jit(_take)/gather | solution.py:42
  36.5 0.9 broadcast_select_fusion
  37.4 0.0 copy-start.4
  37.4 7.7 %all-to-all-start = ((f32[31,32,128]{2,0,1:T(8,128)}), f32[31,32,128]{2,0,1:T(8,128)}, u32[]{:S(2)}, u32[]{:S(2)}) async-start(f32[31,32,128]{2,0,1:T(8,128)} %broadcast_select_fusion), calls=%async_computation | async-start | bytes 1048576 | tf_op jit(solution)/shard_map/all_to_all | solution.py:43
  45.1 1.7 %copy.76 = f32[30,4096]{0,1:T(8,128)S(1)} copy(f32[30,4096]{1,0:T(8,128)} %param.12) | data formatting | bytes 983040 | tf_op args[4]
  46.8 0.0 copy-done.4
  46.8 14.2 %gather_fusion.2 = f32[4096,30]{1,0:T(8,128)} fusion(f32[30,4096]{0,1:T(8,128)S(1)} %copy.76, s32[4096]{0:T(1024)S(1)} %fusion.20), kind=kCustom, calls=%fused_computation.2 | custom fusion | bytes 999424 | tf_op jit(solution)/shard_map/jit(_take)/gather | solution.py:45
  61.0 0.0 copy-start.3
  61.0 3.0 %copy.77 = f32[4096,30]{0,1:T(8,128)} copy(f32[4096,30]{1,0:T(8,128)} %gather_fusion.2) | data formatting | bytes 983040 | tf_op jit(solution)/shard_map/jit(_take)/gather | solution.py:45
  64.0 0.0 copy-done.3
  64.1 0.0 all-to-all-done
  64.1 1.7 %copy.74 = f32[31,32,128]{0,2,1:T(8,128)S(1)} copy(f32[31,32,128]{2,0,1:T(8,128)} %all-to-all-done) | data formatting | bytes 1015808 | tf_op jit(solution)/shard_map/all_to_all | solution.py:43
  65.7 14.2 %gather_fusion.1 = f32[4096,31]{1,0:T(8,128)} fusion(f32[31,4096]{0,1:T(8,128)S(1)} %bitcast.33, s32[4096]{0:T(1024)S(1)} %get-tuple-element.20), kind=kCustom, calls=%fused_computation.1 | custom fusion | bytes 1032192 | tf_op jit(solution)/shard_map/jit(_take)/gather | solution.py:44
  79.9 0.0 copy-start
  79.9 0.0 copy-start.1
  79.9 0.0 copy-start.5
  79.9 2.3 %copy.75 = f32[4096,31]{0,1:T(8,128)S(1)} copy(f32[4096,31]{1,0:T(8,128)} %gather_fusion.1) | data formatting | bytes 1015808 | tf_op jit(solution)/shard_map/jit(_take)/gather | solution.py:44
  82.3 0.0 copy-done
  82.3 0.0 copy-done.1
  82.3 0.0 copy-done.5
  82.4 0.9 broadcast_multiply_fusion
  83.3 2.0 %copy.78 = f32[4096,31]{1,0:T(8,128)} copy(f32[4096,31]{0,1:T(8,128)S(1)} %maximum_bitcast_fusion) | data formatting | bytes 1015808 | tf_op jit(solution)/shard_map/concatenate | solution.py:52
  85.4 23.2 %scatter_custom_fusion = f32[31,4096]{0,1:T(8,128)S(1)} fusion(s32[4096]{0:T(1024)S(1)} %get-tuple-element.21, f32[4096,31]{1,0:T(8,128)} %copy.78, f32[]{:T(128)} %constant.25.clone.1), kind=kCustom, calls=%fused_computation.10 | custom fusion | flops 126976 | bytes 508416 | tf_op jit(solution)/shard_map/scatter-add | solution.py:53
  108.5 1.4 copy.79
  110.0 21.3 %all_to_all.21 = f32[31,32,128]{2,0,1:T(8,128)S(1)} all-to-all(f32[31,32,128]{2,0,1:T(8,128)} %copy.79), channel_id=1, replica_groups=mesh['gx'=8,'gy'=4] {'gx','gy'}, dimensions={1} | all-to-all | bytes 1015808 | tf_op jit(solution)/shard_map/all_to_all | solution.py:54
  131.3 0.3 copy.80
  131.6 0.3 copy.83
  131.9 2.0 %copy.81 = f32[4096,31]{1,0:T(8,128)} copy(f32[4096,31]{0,1:T(8,128)S(1)} %bitcast.38) | data formatting | bytes 1015808 | tf_op jit(solution)/shard_map/all_to_all | solution.py:54
  133.9 22.9 %scatter_custom_fusion.1 = f32[31,2048]{0,1:T(8,128)S(1)} fusion(s32[4096]{0:T(1024)S(1)} %bitcast.42, f32[4096,31]{1,0:T(8,128)} %copy.81, f32[]{:T(128)} %constant.25.clone.1), kind=kCustom, calls=%fused_computation.22 | custom fusion | flops 126976 | bytes 254464 | tf_op jit(solution)/shard_map/scatter-add | solution.py:55
  156.8 0.6 fusion
  157.5 0.3 fusion.1
  157.8 1.0 copy.82
  (11 shorter events, 0.2 us)
Async XLA Ops:
  0.6 18.3 %copy-start.2 = (f32[30,4,4,128]{3,2,1,0:T(4,128)S(1)}, f32[30,4,4,128]{3,2,1,0:T(4,128)}, u32[]{:S(2)}) copy-start(f32[30,4,4,128]{3,2,1,0:T(4,128)} %param.8) | copy-start | bytes 737284
  0.6 18.3 %copy-start.6 = (f32[4,4,128]{2,1,0:T(4,128)S(1)}, f32[4,4,128]{2,1,0:T(4,128)}, u32[]{:S(2)}) copy-start(f32[4,4,128]{2,1,0:T(4,128)} %param.9) | copy-start | bytes 24580
  1.6 6.9 %collective-permute-start.1 = (f32[30,1,4,128]{3,2,1,0:T(4,128)S(1)}, f32[30,1,4,128]{3,2,1,0:T(4,128)S(1)}, u32[]{:S(2)}, u32[]{:S(2)}) collective-permute-start(f32[30,1,4,128]{3,2,1,0:T(4,128)S(1)} %get-tuple-element.19), channel_id=1, source_target_pairs={{0,4},{4,8},{8,12},{12,16},{16,20},{20,24},{24,28},{1,5},{5,9},{9,... | collective-permute-start | bytes 184328 | tf_op jit(solution)/shard_map/ppermute | solution.py:16
  6.4 6.1 %collective-permute-start = (f32[30,1,4,128]{3,2,1,0:T(4,128)S(1)}, f32[30,1,4,128]{3,2,1,0:T(4,128)S(1)}, u32[]{:S(2)}, u32[]{:S(2)}) collective-permute-start(f32[30,1,4,128]{3,2,1,0:T(4,128)S(1)} %get-tuple-element.18), channel_id=1, source_target_pairs={{4,0},{8,4},{12,8},{16,12},{20,16},{24,20},{28,24},{5,1},{9,5},{13... | collective-permute-start | bytes 184328 | tf_op jit(solution)/shard_map/ppermute | solution.py:17
  12.7 4.4 %collective-permute-start.3 = (f32[30,6,1,128]{3,2,1,0:T(1,128)S(1)}, f32[30,6,1,128]{3,2,1,0:T(1,128)S(1)}, u32[]{:S(2)}, u32[]{:S(2)}) collective-permute-start(f32[30,6,1,128]{3,2,1,0:T(1,128)S(1)} %get-tuple-element.17), channel_id=1, source_target_pairs={{0,1},{1,2},{2,3},{4,5},{5,6},{6,7},{8,9},{9,10},{10,11},{12,13},{... | collective-permute-start | bytes 276488 | tf_op jit(solution)/shard_map/ppermute | solution.py:16
  14.0 4.9 %collective-permute-start.2 = (f32[30,6,1,128]{3,2,1,0:T(1,128)S(1)}, f32[30,6,1,128]{3,2,1,0:T(1,128)S(1)}, u32[]{:S(2)}, u32[]{:S(2)}) collective-permute-start(f32[30,6,1,128]{3,2,1,0:T(1,128)S(1)} %get-tuple-element.16), channel_id=1, source_target_pairs={{1,0},{2,1},{3,2},{5,4},{6,5},{7,6},{9,8},{10,9},{11,10},{13,12},{... | collective-permute-start | bytes 276488 | tf_op jit(solution)/shard_map/ppermute | solution.py:17
  37.4 9.4 %copy-start.4 = (s32[4096]{0:T(1024)S(1)}, s32[4096]{0:T(1024)}, u32[]{:S(2)}) copy-start(s32[4096]{0:T(1024)} %param.15) | copy-start | bytes 49156
  37.4 26.7 %all-to-all-start = ((f32[31,32,128]{2,0,1:T(8,128)}), f32[31,32,128]{2,0,1:T(8,128)}, u32[]{:S(2)}, u32[]{:S(2)}) async-start(f32[31,32,128]{2,0,1:T(8,128)} %broadcast_select_fusion), calls=%async_computation | async-start | bytes 1048576 | tf_op jit(solution)/shard_map/all_to_all | solution.py:43
  61.0 3.0 %copy-start.3 = (s32[4096]{0:T(1024)S(1)}, s32[4096]{0:T(1024)}, u32[]{:S(2)}) copy-start(s32[4096]{0:T(1024)} %param.14) | copy-start | bytes 49156
  79.9 2.4 %copy-start = (f32[30,4096]{1,0:T(8,128)S(1)}, f32[30,4096]{1,0:T(8,128)}, u32[]{:S(2)}) copy-start(f32[30,4096]{1,0:T(8,128)} %param.12) | copy-start | bytes 1474564
  79.9 2.4 %copy-start.1 = (f32[4096,30]{0,1:T(8,128)S(1)}, f32[4096,30]{0,1:T(8,128)}, u32[]{:S(2)}) copy-start(f32[4096,30]{0,1:T(8,128)} %copy.77) | copy-start | bytes 1474564
  79.9 2.4 %copy-start.5 = (f32[4096]{0:T(1024)S(1)}, f32[4096]{0:T(1024)}, u32[]{:S(2)}) copy-start(f32[4096]{0:T(1024)} %param.13) | copy-start | bytes 49156
where the time goes:
time: 160 us; the launch traced here: 159 us
  local copies, waits for them, and re-layouts  64 us (40%)
  other arithmetic  51.3 us (32%)
  blocking collectives  21.3 us (13%)
  starting transfers between devices  16.5 us (10%)
  waiting for transfers between devices  4.86 us (3%)
    scatter-add x1, other arithmetic, on_device(): jnp.zeros((species + 1, slot_count), jnp.float32).at[:, particle_slots]  23.2 us
    scatter-add x1, other arithmetic, on_device(): jnp.zeros((species + 1, cell_count), jnp.float32).at[:, flat_list]  22.9 us
    all_to_all x1, blocking collectives, on_device(): lax.all_to_all(moments, ('gx', 'gy'), split_axis=1, concat_axis=1, tiled=...  21.3 us
    gather x2, local copies, waits for them, and re-layouts, on_device(): mates = jnp.take(compositions, partners, axis=1)  17.2 us
    gather x2, local copies, waits for them, and re-layouts, on_device(): local_means = jnp.take(received, particle_slots, axis=1)  16.5 us
    gather x2, local copies, waits for them, and re-layouts, on_device(): outgoing = jnp.take(fields, flat_list, axis=1)  16.4 us
    all_to_all x1, starting transfers between devices, on_device(): lax.all_to_all(outgoing, ('gx', 'gy'), split_axis=1, concat_axis=1, tiled...  7.72 us
    ppermute x2, starting transfers between devices, with_halo(): before = lax.ppermute(last, axis, up)  6.17 us
  transfers between devices with their start and end apart: 5, of which 2 were waited for; matrix products, arithmetic and copies ran while one was open for 14% of the time, Pallas kernels for 0%

commit v1 on v0

--- a/solution.py
+++ b/solution.py
@@ -40,7 +40,12 @@
     slot_count = groups_x * groups_y * slots_peer
     flat_list = send_lists[0].reshape(-1)
     outgoing = jnp.take(fields, flat_list, axis=1)
-    received = lax.all_to_all(outgoing, ("gx", "gy"), split_axis=1, concat_axis=1, tiled=True)
+    received = jnp.concatenate(
+        lax.all_to_all(
+            jnp.stack(jnp.split(outgoing, lax.axis_size(("gx", "gy")), axis=1)), ("gx", "gy"), 0, 0
+        ),
+        axis=1,
+    )
     local_means = jnp.take(received, particle_slots, axis=1)
     mates = jnp.take(compositions, partners, axis=1)
     blend_rate = 1.0 - jnp.exp(-local_means[species])

time: 160 us -> 178 us (1.11)
  local copies, waits for them, and re-layouts: 64 us -> 83.1 us
    unnamed x20 -> x51, local copies, waits for them, and re-layouts: 4.07 us -> 22.7 us
  transfers between devices with their start and end apart: 5 -> 5, of which waited for: 2 -> 2; matrix products, arithmetic and copies ran while one was open for 14% -> 13% of each run, Pallas kernels for 0% -> 0%
where the time goes in v1:
time: 178 us; the launch traced here: 177 us
  local copies, waits for them, and re-layouts  83.1 us (47%)
  other arithmetic  51.2 us (29%)
  blocking collectives  21.3 us (12%)
  starting transfers between devices  16.5 us (9%)
  waiting for transfers between devices  4.14 us (2%)
    scatter-add x1, other arithmetic, on_device(): jnp.zeros((species + 1, slot_count), jnp.float32).at[:, particle_slots]  23.2 us
    scatter-add x1, other arithmetic, on_device(): jnp.zeros((species + 1, cell_count), jnp.float32).at[:, flat_list]  22.9 us
    unnamed x51, local copies, waits for them, and re-layouts  22.7 us
    all_to_all x1, blocking collectives, on_device(): lax.all_to_all(moments, ('gx', 'gy'), split_axis=1, concat_axis=1, tiled=...  21.3 us
    gather x2, local copies, waits for them, and re-layouts, on_device(): mates = jnp.take(compositions, partners, axis=1)  17.1 us
    gather x2, local copies, waits for them, and re-layouts, on_device(): local_means = jnp.take(received, particle_slots, axis=1)  16.4 us
    gather x2, local copies, waits for them, and re-layouts, on_device(): outgoing = jnp.take(fields, flat_list, axis=1)  16.3 us
    all_to_all x1, starting transfers between devices, on_device(): lax.all_to_all(jnp.stack(jnp.split(outgoing, lax.axis_size(('gx', 'gy')),...  7.72 us
  transfers between devices with their start and end apart: 5, of which 2 were waited for; matrix products, arithmetic and copies ran while one was open for 13% of the time, Pallas kernels for 0%

profile of v1, /device:TPU:0, one launch (start us, length us, event | category | flops | bytes accessed | tf_op | source)
XLA Modules:
  0.0 177.1 jit_solution(9691389291501184115)
XLA Ops:
  0.7 0.9 fusion.23
  1.6 4.9 %collective-permute-start.1 = (f32[30,1,4,128]{3,2,1,0:T(4,128)S(1)}, f32[30,1,4,128]{3,2,1,0:T(4,128)S(1)}, u32[]{:S(2)}, u32[]{:S(2)}) collective-permute-start(f32[30,1,4,128]{3,2,1,0:T(4,128)S(1)} %get-tuple-element.19), channel_id=1, source_target_pairs={{0,4},{4,8},{8,12},{12,16},{16,20},{20,24},{24,28},{1,5},{5,9},{9,... | collective-permute-start | bytes 184328 | tf_op jit(solution)/shard_map/ppermute | solution.py:16
  6.4 1.3 collective-permute-start
  7.7 0.7 compare_select_fusion
  8.5 0.7 fusion.20
  9.3 1.0 constant_dynamic-update-slice_fusion.1
  10.2 2.3 %collective-permute-done = f32[30,1,4,128]{3,2,1,0:T(4,128)S(1)} collective-permute-done((f32[30,1,4,128]{3,2,1,0:T(4,128)S(1)}, f32[30,1,4,128]{3,2,1,0:T(4,128)S(1)}, u32[]{:S(2)}, u32[]{:S(2)}) %collective-permute-start) | collective-permute-done | bytes 61472 | tf_op jit(solution)/shard_map/ppermute | solution.py:17
  12.7 1.3 collective-permute-start.3
  14.0 1.3 collective-permute-start.2
  15.3 0.7 compare_and_fusion.1
  16.1 1.1 copy.136
  17.1 1.8 %collective-permute-done.2 = f32[30,6,1,128]{3,2,1,0:T(1,128)S(1)} collective-permute-done((f32[30,6,1,128]{3,2,1,0:T(1,128)S(1)}, f32[30,6,1,128]{3,2,1,0:T(1,128)S(1)}, u32[]{:S(2)}, u32[]{:S(2)}) %collective-permute-start.2) | collective-permute-done | bytes 92192 | tf_op jit(solution)/shard_map/ppermute | solution.py:17
  19.0 0.4 fusion.14
  19.4 0.4 copy.135
  20.1 14.1 %gather_fusion = f32[4096,31]{1,0:T(8,128)} fusion(f32[31,2048]{0,1:T(8,128)S(1)} %pad_maximum_fusion, s32[4096]{0:T(1024)S(1)} %get-tuple-element.23), kind=kCustom, calls=%fused_computation | custom fusion | bytes 1032192 | tf_op jit(solution)/shard_map/jit(_take)/gather | solution.py:42
  34.2 2.2 %copy.137 = f32[4096,31]{0,1:T(8,128)S(1)} copy(f32[4096,31]{1,0:T(8,128)} %gather_fusion) | data formatting | bytes 1015808 | tf_op jit(solution)/shard_map/jit(_take)/gather | solution.py:42
  36.5 0.6 constant_dynamic-update-slice_fusion.34
  37.1 0.6 constant_dynamic-update-slice_fusion.33
  37.7 0.6 constant_dynamic-update-slice_fusion.32
  38.3 0.6 constant_dynamic-update-slice_fusion.31
  38.9 0.6 constant_dynamic-update-slice_fusion.30
  39.5 0.6 constant_dynamic-update-slice_fusion.29
  40.1 0.6 constant_dynamic-update-slice_fusion.28
  40.7 0.6 constant_dynamic-update-slice_fusion.27
  41.3 0.6 constant_dynamic-update-slice_fusion.26
  41.9 0.6 constant_dynamic-update-slice_fusion.25
  42.5 0.6 constant_dynamic-update-slice_fusion.24
  43.1 0.6 constant_dynamic-update-slice_fusion.23
  43.7 0.6 constant_dynamic-update-slice_fusion.22
  44.3 0.6 constant_dynamic-update-slice_fusion.21
  44.9 0.6 constant_dynamic-update-slice_fusion.20
  45.5 0.6 constant_dynamic-update-slice_fusion.19
  46.1 0.6 constant_dynamic-update-slice_fusion.18
  46.7 0.6 constant_dynamic-update-slice_fusion.17
  47.4 0.6 constant_dynamic-update-slice_fusion.16
  48.0 0.6 constant_dynamic-update-slice_fusion.15
  48.6 0.6 constant_dynamic-update-slice_fusion.14
  49.2 0.6 constant_dynamic-update-slice_fusion.13
  49.8 0.6 constant_dynamic-update-slice_fusion.12
  50.3 0.6 constant_dynamic-update-slice_fusion.11
  51.0 0.6 constant_dynamic-update-slice_fusion.10
  51.6 0.6 constant_dynamic-update-slice_fusion.9
  52.2 0.6 constant_dynamic-update-slice_fusion.8
  52.8 0.6 constant_dynamic-update-slice_fusion.7
  53.4 0.6 constant_dynamic-update-slice_fusion.6
  54.0 0.6 constant_dynamic-update-slice_fusion.5
  54.6 0.6 constant_dynamic-update-slice_fusion.4
  55.2 0.6 constant_dynamic-update-slice_fusion.3
  55.8 7.7 %all-to-all-start = ((f32[32,31,128]{2,1,0:T(8,128)}), f32[32,31,128]{2,1,0:T(8,128)}, u32[]{:S(2)}, u32[]{:S(2)}) async-start(f32[32,31,128]{2,1,0:T(8,128)} %constant_dynamic-update-slice_fusion.3), calls=%async_computation | async-start | bytes 1048576 | tf_op jit(solution)/shard_map/all_to_all | solution.py:44
  63.5 1.7 copy.140
  65.2 14.1 %gather_fusion.2 = f32[4096,30]{1,0:T(8,128)} fusion(f32[30,4096]{0,1:T(8,128)S(1)} %copy.140, s32[4096]{0:T(1024)S(1)} %get-tuple-element.22), kind=kCustom, calls=%fused_computation.2 | custom fusion | bytes 999424 | tf_op jit(solution)/shard_map/jit(_take)/gather | solution.py:50
  79.3 3.0 %copy.141 = f32[4096,30]{0,1:T(8,128)} copy(f32[4096,30]{1,0:T(8,128)} %gather_fusion.2) | data formatting | bytes 983040 | tf_op jit(solution)/shard_map/jit(_take)/gather | solution.py:50
  82.4 1.7 copy.138
  84.0 14.1 %gather_fusion.1 = f32[4096,31]{1,0:T(8,128)} fusion(f32[31,4096]{0,1:T(8,128)S(1)} %bitcast.161, s32[4096]{0:T(1024)S(1)} %get-tuple-element.20), kind=kCustom, calls=%fused_computation.1 | custom fusion | bytes 1032192 | tf_op jit(solution)/shard_map/jit(_take)/gather | solution.py:49
  98.2 2.3 %copy.139 = f32[4096,31]{0,1:T(8,128)S(1)} copy(f32[4096,31]{1,0:T(8,128)} %gather_fusion.1) | data formatting | bytes 1015808 | tf_op jit(solution)/shard_map/jit(_take)/gather | solution.py:49
  100.6 0.9 broadcast_multiply_fusion
  101.6 2.0 %copy.142 = f32[4096,31]{1,0:T(8,128)} copy(f32[4096,31]{0,1:T(8,128)S(1)} %maximum_bitcast_fusion) | data formatting | bytes 1015808 | tf_op jit(solution)/shard_map/concatenate | solution.py:57
  103.6 23.2 %scatter_custom_fusion = f32[31,4096]{0,1:T(8,128)S(1)} fusion(s32[4096]{0:T(1024)S(1)} %get-tuple-element.21, f32[4096,31]{1,0:T(8,128)} %copy.142, f32[]{:T(128)} %constant.25.clone.1), kind=kCustom, calls=%fused_computation.10 | custom fusion | flops 126976 | bytes 508416 | tf_op jit(solution)/shard_map/scatter-add | solution.py:58
  126.8 1.4 copy.143
  128.2 21.3 %all_to_all.17 = f32[31,32,128]{2,0,1:T(8,128)S(1)} all-to-all(f32[31,32,128]{2,0,1:T(8,128)} %copy.143), channel_id=1, replica_groups=mesh['gx'=8,'gy'=4] {'gx','gy'}, dimensions={1} | all-to-all | bytes 1015808 | tf_op jit(solution)/shard_map/all_to_all | solution.py:59
  150.2 2.0 %copy.145 = f32[4096,31]{1,0:T(8,128)} copy(f32[4096,31]{0,1:T(8,128)S(1)} %bitcast.165) | data formatting | bytes 1015808 | tf_op jit(solution)/shard_map/all_to_all | solution.py:59
  152.2 22.9 %scatter_custom_fusion.1 = f32[31,2048]{0,1:T(8,128)S(1)} fusion(s32[4096]{0:T(1024)S(1)} %bitcast.169, f32[4096,31]{1,0:T(8,128)} %copy.145, f32[]{:T(128)} %constant.25.clone.1), kind=kCustom, calls=%fused_computation.23 | custom fusion | flops 126976 | bytes 254464 | tf_op jit(solution)/shard_map/scatter-add | solution.py:60
  175.1 0.6 fusion
  176.1 1.0 copy.146
  (32 shorter events, 1.7 us)
Async XLA Ops:
  0.6 18.3 %copy-start.2 = (f32[30,4,4,128]{3,2,1,0:T(4,128)S(1)}, f32[30,4,4,128]{3,2,1,0:T(4,128)}, u32[]{:S(2)}) copy-start(f32[30,4,4,128]{3,2,1,0:T(4,128)} %param.8) | copy-start | bytes 737284
  0.6 18.3 %copy-start.6 = (f32[4,4,128]{2,1,0:T(4,128)S(1)}, f32[4,4,128]{2,1,0:T(4,128)}, u32[]{:S(2)}) copy-start(f32[4,4,128]{2,1,0:T(4,128)} %param.9) | copy-start | bytes 24580
  1.6 7.7 %collective-permute-start.1 = (f32[30,1,4,128]{3,2,1,0:T(4,128)S(1)}, f32[30,1,4,128]{3,2,1,0:T(4,128)S(1)}, u32[]{:S(2)}, u32[]{:S(2)}) collective-permute-start(f32[30,1,4,128]{3,2,1,0:T(4,128)S(1)} %get-tuple-element.19), channel_id=1, source_target_pairs={{0,4},{4,8},{8,12},{12,16},{16,20},{20,24},{24,28},{1,5},{5,9},{9,... | collective-permute-start | bytes 184328 | tf_op jit(solution)/shard_map/ppermute | solution.py:16
  6.4 6.1 %collective-permute-start = (f32[30,1,4,128]{3,2,1,0:T(4,128)S(1)}, f32[30,1,4,128]{3,2,1,0:T(4,128)S(1)}, u32[]{:S(2)}, u32[]{:S(2)}) collective-permute-start(f32[30,1,4,128]{3,2,1,0:T(4,128)S(1)} %get-tuple-element.18), channel_id=1, source_target_pairs={{4,0},{8,4},{12,8},{16,12},{20,16},{24,20},{28,24},{5,1},{9,5},{13... | collective-permute-start | bytes 184328 | tf_op jit(solution)/shard_map/ppermute | solution.py:17
  12.7 4.4 %collective-permute-start.3 = (f32[30,6,1,128]{3,2,1,0:T(1,128)S(1)}, f32[30,6,1,128]{3,2,1,0:T(1,128)S(1)}, u32[]{:S(2)}, u32[]{:S(2)}) collective-permute-start(f32[30,6,1,128]{3,2,1,0:T(1,128)S(1)} %get-tuple-element.17), channel_id=1, source_target_pairs={{0,1},{1,2},{2,3},{4,5},{5,6},{6,7},{8,9},{9,10},{10,11},{12,13},{... | collective-permute-start | bytes 276488 | tf_op jit(solution)/shard_map/ppermute | solution.py:16
  14.0 4.9 %collective-permute-start.2 = (f32[30,6,1,128]{3,2,1,0:T(1,128)S(1)}, f32[30,6,1,128]{3,2,1,0:T(1,128)S(1)}, u32[]{:S(2)}, u32[]{:S(2)}) collective-permute-start(f32[30,6,1,128]{3,2,1,0:T(1,128)S(1)} %get-tuple-element.16), channel_id=1, source_target_pairs={{1,0},{2,1},{3,2},{5,4},{6,5},{7,6},{9,8},{10,9},{11,10},{13,12},{... | collective-permute-start | bytes 276488 | tf_op jit(solution)/shard_map/ppermute | solution.py:17
  55.8 26.6 %all-to-all-start = ((f32[32,31,128]{2,1,0:T(8,128)}), f32[32,31,128]{2,1,0:T(8,128)}, u32[]{:S(2)}, u32[]{:S(2)}) async-start(f32[32,31,128]{2,1,0:T(8,128)} %constant_dynamic-update-slice_fusion.3), calls=%async_computation | async-start | bytes 1048576 | tf_op jit(solution)/shard_map/all_to_all | solution.py:44
  79.3 3.0 %copy-start.4 = (s32[4096]{0:T(1024)S(1)}, s32[4096]{0:T(1024)}, u32[]{:S(2)}) copy-start(s32[4096]{0:T(1024)} %param.15) | copy-start | bytes 49156
  79.3 3.0 %copy-start.3 = (s32[4096]{0:T(1024)S(1)}, s32[4096]{0:T(1024)}, u32[]{:S(2)}) copy-start(s32[4096]{0:T(1024)} %param.14) | copy-start | bytes 49156
  98.2 2.4 %copy-start = (f32[30,4096]{1,0:T(8,128)S(1)}, f32[30,4096]{1,0:T(8,128)}, u32[]{:S(2)}) copy-start(f32[30,4096]{1,0:T(8,128)} %param.12) | copy-start | bytes 1474564
  98.2 2.4 %copy-start.1 = (f32[4096,30]{0,1:T(8,128)S(1)}, f32[4096,30]{0,1:T(8,128)}, u32[]{:S(2)}) copy-start(f32[4096,30]{0,1:T(8,128)} %copy.141) | copy-start | bytes 1474564
  98.2 2.4 %copy-start.5 = (f32[4096]{0:T(1024)S(1)}, f32[4096]{0:T(1024)}, u32[]{:S(2)}) copy-start(f32[4096]{0:T(1024)} %param.13) | copy-start | bytes 49156
